TPU v7x, 256 devices: a whole 4x4x8 slice. The times are simulated.
256 devices in a mesh: bead: 16 (over z, core), atom: 16 (over x, y).
Axes of the slice: x: 4, y: 4, z: 8, core: 2. Of those that a mesh axis runs over, the one named last changes fastest.
Arguments:
- positions: float32 [64, 3, 16384], P('bead', None, 'atom'), may hold values from -6 to 6
- momenta: float32 [64, 3, 16384], P('bead', None, 'atom'), may hold values from -6 to 6
- charge: float32 [16384], P('atom'), may hold values from -1 to 1
- masses: float32 [16384], P('atom'), may hold values from 0.5 to 4
- pair_local: int32 [512], P('atom'), may hold values from 0 to 127, as said below
- pair_other: int32 [512], P('atom'), may hold values from 0 to 127, as said below
- pair_count: int32 [16], P('atom'), may hold values from 0 to 32, as said below
Outputs:
- new_positions: float32 [64, 3, 16384], P('bead', None, 'atom')
- new_momenta: float32 [64, 3, 16384], P('bead', None, 'atom')
- spring: float32 [16384], P('atom')
Inputs may be any that keep to these rules, and one draw needn't show every extreme that they name: `pair_local`: the slots of atom block d (slots d * 32 to (d + 1) * 32 - 1) name tiles of that block: d * 8 to (d + 1) * 8 - 1. `pair_other`: each slot's neighbour tile lies within 8 tiles of its tile, counting cyclically over 128 tiles. `pair_count`: the counts of blocks d and d + 8 sum to at most 32.
All inputs are finite; a program needn't handle non-finite values.
Results may differ from a plain program's by a relative error of at most 0.000071.
Values sent between devices are 32-bit elements; how exact they have to be, the bound alone decides.
No kernel may reach another device: no remote copies, remote signals or barrier semaphores. Data moves between devices by JAX's collectives and lax.ppermute only.
A program may use at most 64 MiB of HBM per device.

v0:
```python
import jax
import jax.numpy as jnp
from jax import lax
from jax.sharding import PartitionSpec as P

time_step = 1.0
omega_cycle = 1.2
width_sq = 2.0


def extended(block, sides, width):
    for axis, dim in sides:
        count = lax.axis_size(axis)
        forward = [(i, i + 1) for i in range(count - 1)]
        forward.append((count - 1, 0))
        backward = [(target, source) for source, target in forward]
        low = lax.ppermute(
            lax.slice_in_dim(block, block.shape[dim] - width, None, axis=dim), axis, forward
        )
        high = lax.ppermute(lax.slice_in_dim(block, 0, width, axis=dim), axis, backward)
        block = jnp.concatenate([low, block, high], axis=dim)
    return block


def sent_to_all(x, axis):
    peers = lax.axis_size(axis)
    return lax.all_to_all(jnp.broadcast_to(x[None], (peers, *x.shape)), axis, 0, 0, tiled=True)


def in_order(blocks, dim):
    blocks = jnp.moveaxis(blocks, 0, dim)
    shape = blocks.shape
    return blocks.reshape(*shape[:dim], shape[dim] * shape[dim + 1], *shape[dim + 2 :])


def gathered_copies(x, axis, dim):
    blocks = sent_to_all(x, axis)
    return in_order(blocks, dim)


def cycle_table(beads):
    bead_index = jnp.arange(beads, dtype=jnp.float32)[:, None]
    mode_index = jnp.arange(beads, dtype=jnp.float32)[None, :]
    middle = beads // 2
    angle = 2.0 * jnp.pi * bead_index * mode_index / beads
    cosine_part = jnp.sqrt(2.0 / beads) * jnp.cos(angle)
    sine_part = jnp.sqrt(2.0 / beads) * jnp.sin(angle)
    edge_part = jnp.sqrt(1.0 / beads) * jnp.cos(jnp.pi * bead_index)
    first = jnp.sqrt(1.0 / beads) * jnp.ones_like(angle)
    table = jnp.where(
        mode_index == 0,
        first,
        jnp.where(
            mode_index < middle, cosine_part, jnp.where(mode_index == middle, edge_part, sine_part)
        ),
    )
    frequency = 2.0 * omega_cycle * jnp.sin(jnp.pi * jnp.arange(beads, dtype=jnp.float32) / beads)
    return (table, frequency)


def pair_force(left_pos, right_pos, left_charge, right_charge):
    separation = left_pos[..., :, None] - right_pos[..., None, :]
    dist_sq = jnp.sum(separation * separation, axis=-3)
    weights = (
        left_charge[..., :, None]
        * right_charge[..., None, :]
        * jnp.exp(-dist_sq / (2.0 * width_sq))
        / width_sq
    )
    return jnp.sum(separation * weights[..., None, :, :], axis=-1)


def propagate(mode_pos, mode_mom, frequency, masses, beads):
    freq_col = frequency[:, None, None]
    mass_row = masses[None, None, :]
    cosine = jnp.cos(freq_col * time_step)
    sine = jnp.sin(freq_col * time_step)
    reach = jnp.where(freq_col > 0, sine / jnp.where(freq_col > 0, freq_col, 1.0), time_step)
    moved_pos = cosine * mode_pos + reach * mode_mom / mass_row
    moved_mom = -mass_row * freq_col * sine * mode_pos + cosine * mode_mom
    spring = (
        jnp.sum(0.5 * mass_row * freq_col * freq_col * moved_pos * moved_pos, axis=(0, 1)) / beads
    )
    return (moved_pos, moved_mom, spring)


def slot_forces(packed):
    slots = packed.shape[0]
    blocks = packed.reshape((slots // 4, 4) + packed.shape[1:])

    def one_block(block_pack):
        return pair_force(
            block_pack[:, 0, :, :3],
            block_pack[:, 1, :, :3],
            block_pack[:, 0, :, 3],
            block_pack[:, 1, :, 3],
        )

    result = lax.map(one_block, blocks)
    return result.reshape((slots,) + result.shape[2:])


def on_device(positions, momenta, charge, masses, pair_local, pair_other, pair_count):
    bead_dev, _, atom_dev = positions.shape
    tile_atoms = 128
    tile_dev = atom_dev // tile_atoms
    atom_count = lax.axis_size("atom")
    bead_count = lax.axis_size("bead")
    beads = bead_dev * bead_count
    tiles = tile_dev * atom_count
    slots = pair_local.shape[0]
    hp = lax.Precision.HIGHEST
    table, frequency = cycle_table(beads)
    sub_atoms = atom_dev // bead_count
    gathered_pos = lax.all_to_all(positions, "bead", split_axis=2, concat_axis=0, tiled=True)
    charge_rows = jnp.broadcast_to(charge[None, None, :], (bead_dev, 1, atom_dev))
    packed = jnp.concatenate([positions, charge_rows], axis=1)
    haloed = extended(packed, (("atom", 2),), atom_dev)
    ext_tiles = jnp.transpose(haloed.reshape(bead_dev, 4, 3 * tile_dev, tile_atoms), (2, 0, 1, 3))
    base_tile = lax.axis_index("atom") * tile_dev - tile_dev
    left_local = (pair_local - base_tile) % tiles
    right_local = (pair_other - base_tile) % tiles
    live_count = pair_count[0]
    slot_ids = jnp.arange(slots)
    live_mask = (slot_ids < live_count).astype(jnp.float32)
    left_block = jnp.take(ext_tiles, left_local, axis=0)
    right_block = jnp.take(ext_tiles, right_local, axis=0)
    left_block = jnp.concatenate(
        [left_block[:, :, :3], left_block[:, :, 3:] * live_mask[:, None, None, None]], axis=2
    )
    forces = slot_forces(jnp.stack([left_block, right_block], axis=1))
    onehot = (left_local[None, :] - tile_dev == jnp.arange(tile_dev)[:, None]).astype(jnp.float32)
    summed = jnp.einsum("ts,sbca->bcta", onehot, forces, precision=hp)
    force = summed.reshape(bead_dev, 3, atom_dev)
    kicked = momenta + 0.5 * time_step * force
    gathered_mom = lax.all_to_all(kicked, "bead", split_axis=2, concat_axis=0, tiled=True)
    mode_pos = jnp.einsum("jk,jca->kca", table, gathered_pos, precision=hp)
    mode_mom = jnp.einsum("jk,jca->kca", table, gathered_mom, precision=hp)
    sub_masses = lax.dynamic_slice_in_dim(masses, lax.axis_index("bead") * sub_atoms, sub_atoms, 0)
    moved_pos, moved_mom, spring_sub = propagate(mode_pos, mode_mom, frequency, sub_masses, beads)
    stacked = jnp.stack([moved_pos, moved_mom], axis=1)
    returned_rows = jnp.einsum("jk,kxca->jxca", table, stacked, precision=hp)
    result = lax.all_to_all(returned_rows, "bead", split_axis=0, concat_axis=3, tiled=True)
    spring = gathered_copies(spring_sub, "bead", 0)
    return (result[:, 0], result[:, 1], spring)


def solution(mesh):
    return jax.shard_map(
        on_device,
        mesh=mesh,
        in_specs=(
            P("bead", None, "atom"),
            P("bead", None, "atom"),
            P("atom"),
            P("atom"),
            P("atom"),
            P("atom"),
            P("atom"),
        ),
        out_specs=(P("bead", None, "atom"), P("bead", None, "atom"), P("atom")),
        check_vma=False,
    )
```

profile of v0, /device:TPU:1, one launch (start us, length us, event | category | flops | bytes accessed | tf_op | source)
XLA Modules:
  0.0 99.7 jit_solution(16731278039876479121)
XLA Ops:
  0.6 0.7 broadcast_in_dim.92
  1.3 0.8 pad_maximum_fusion.3
  2.2 2.2 %collective-permute-start = (f32[4,4,1024]{2,0,1:T(4,128)S(1)}, f32[4,4,1024]{2,0,1:T(4,128)S(1)}, u32[]{:S(2)}, u32[]{:S(2)}) collective-permute-start(f32[4,4,1024]{2,0,1:T(4,128)S(1)} %pad_maximum_fusion.3), channel_id=1, source_target_pairs={{0,1},{1,2},{2,3},{3,4},{4,5},{5,6},{6,7},{7,8},{8,9},{9,10},{10,1... | collective-permute-start | bytes 196616 | tf_op jit(solution)/shard_map/ppermute | solution.py:17
  4.4 3.7 %collective-permute-start.1 = (f32[4,4,1024]{2,0,1:T(4,128)S(1)}, f32[4,4,1024]{2,0,1:T(4,128)S(1)}, u32[]{:S(2)}, u32[]{:S(2)}) collective-permute-start(f32[4,4,1024]{2,0,1:T(4,128)S(1)} %pad_maximum_fusion.3), channel_id=1, source_target_pairs={{1,0},{2,1},{3,2},{4,3},{5,4},{6,5},{7,6},{8,7},{9,8},{10,9},{11,1... | collective-permute-start | bytes 196616 | tf_op jit(solution)/shard_map/ppermute | solution.py:20
  8.1 1.6 %copy.67 = f32[4,3,1024]{0,1,2:T(4,128)S(1)} copy(f32[4,3,1024]{2,0,1:T(4,128)} %param.11) | data formatting | bytes 98304 | tf_op args[0]
  9.7 1.9 %reshape.245 = f32[16,1,768]{2,1,0:T(1,128)} reshape(f32[1024,3,4]{2,1,0:T(4,128)S(1)} %bitcast.90) | data formatting | bytes 98304
  11.6 9.5 %all-to-all-start = ((f32[16,1,768]{2,1,0:T(1,128)}), f32[16,1,768]{2,1,0:T(1,128)S(1)}, u32[]{:S(2)}, u32[]{:S(2)}) async-start(f32[16,1,768]{2,1,0:T(1,128)} %reshape.245), calls=%async_computation | async-start | bytes 98304 | tf_op jit(solution)/shard_map/all_to_all | solution.py:115
  22.1 0.8 broadcast_multiply_fusion.1
  23.2 0.7 gather_fusion
  24.4 0.7 gather_fusion.1
  25.5 27.1 %while.10 = (s32[]{:T(128)}, f32[8,4,4,3,128]{4,3,2,1,0:T(4,128)S(1)}, f32[8,4,2,4,4,128]{5,3,1,4,2,0:T(4,128)S(1)}, s32[]{:T(128)}) while((s32[]{:T(128)}, f32[8,4,4,3,128]{4,3,2,1,0:T(4,128)S(1)}, f32[8,4,2,4,4,128]{5,3,1,4,2,0:T(4,128)S(1)}, s32[]{:T(128)}) %tuple.40), condition=%wide.region_3.5_spmd, body=%wide.region_0.4_spmd.sunk | while | flops 5761026 | bytes 4759613 | solution.py:99
  25.6 1.0 %fusion.62 = f32[4,4,128,128]{3,2,1,0:T(8,128)S(1)} fusion(f32[4,4,3,128]{3,2,1,0:T(4,128)S(1)} %copy.97, f32[4,4,3,128]{3,2,1,0:T(4,128)S(1)} %copy.98), kind=kLoop, calls=%fused_computation.4.clone.1 | loop fusion | flops 2097152 | bytes 1097728 | tf_op jit(solution)/shard_map/while/body/eval_jaxpr/reduce_sum | solution.py:63
  27.0 1.9 %fusion.63 = f32[4,4,3,128]{3,2,1,0:T(4,128)S(1)} fusion(f32[4,4,128,128]{3,2,1,0:T(8,128)S(1)} %multiply_multiply_fusion.5, f32[4,4,3,128]{3,2,1,0:T(4,128)S(1)} %copy.97, f32[4,4,3,128]{3,2,1,0:T(4,128)S(1)} %copy.98), kind=kLoop, calls=%fused_computation.5.clone.1 | loop fusion | flops 2353152 | bytes 1122304 | tf_op jit(solution)/shard_map/while/body/eval_jaxpr/reduce_sum | solution.py:70
  29.0 1.0 %fusion.62 = f32[4,4,128,128]{3,2,1,0:T(8,128)S(1)} fusion(f32[4,4,3,128]{3,2,1,0:T(4,128)S(1)} %copy.97, f32[4,4,3,128]{3,2,1,0:T(4,128)S(1)} %copy.98), kind=kLoop, calls=%fused_computation.4.clone.1 | loop fusion | flops 2097152 | bytes 1097728 | tf_op jit(solution)/shard_map/while/body/eval_jaxpr/reduce_sum | solution.py:63
  30.4 1.9 %fusion.63 = f32[4,4,3,128]{3,2,1,0:T(4,128)S(1)} fusion(f32[4,4,128,128]{3,2,1,0:T(8,128)S(1)} %multiply_multiply_fusion.5, f32[4,4,3,128]{3,2,1,0:T(4,128)S(1)} %copy.97, f32[4,4,3,128]{3,2,1,0:T(4,128)S(1)} %copy.98), kind=kLoop, calls=%fused_computation.5.clone.1 | loop fusion | flops 2353152 | bytes 1122304 | tf_op jit(solution)/shard_map/while/body/eval_jaxpr/reduce_sum | solution.py:70
  32.4 1.0 %fusion.62 = f32[4,4,128,128]{3,2,1,0:T(8,128)S(1)} fusion(f32[4,4,3,128]{3,2,1,0:T(4,128)S(1)} %copy.97, f32[4,4,3,128]{3,2,1,0:T(4,128)S(1)} %copy.98), kind=kLoop, calls=%fused_computation.4.clone.1 | loop fusion | flops 2097152 | bytes 1097728 | tf_op jit(solution)/shard_map/while/body/eval_jaxpr/reduce_sum | solution.py:63
  33.8 1.9 %fusion.63 = f32[4,4,3,128]{3,2,1,0:T(4,128)S(1)} fusion(f32[4,4,128,128]{3,2,1,0:T(8,128)S(1)} %multiply_multiply_fusion.5, f32[4,4,3,128]{3,2,1,0:T(4,128)S(1)} %copy.97, f32[4,4,3,128]{3,2,1,0:T(4,128)S(1)} %copy.98), kind=kLoop, calls=%fused_computation.5.clone.1 | loop fusion | flops 2353152 | bytes 1122304 | tf_op jit(solution)/shard_map/while/body/eval_jaxpr/reduce_sum | solution.py:70
  35.7 1.0 %fusion.62 = f32[4,4,128,128]{3,2,1,0:T(8,128)S(1)} fusion(f32[4,4,3,128]{3,2,1,0:T(4,128)S(1)} %copy.97, f32[4,4,3,128]{3,2,1,0:T(4,128)S(1)} %copy.98), kind=kLoop, calls=%fused_computation.4.clone.1 | loop fusion | flops 2097152 | bytes 1097728 | tf_op jit(solution)/shard_map/while/body/eval_jaxpr/reduce_sum | solution.py:63
  37.2 1.9 %fusion.63 = f32[4,4,3,128]{3,2,1,0:T(4,128)S(1)} fusion(f32[4,4,128,128]{3,2,1,0:T(8,128)S(1)} %multiply_multiply_fusion.5, f32[4,4,3,128]{3,2,1,0:T(4,128)S(1)} %copy.97, f32[4,4,3,128]{3,2,1,0:T(4,128)S(1)} %copy.98), kind=kLoop, calls=%fused_computation.5.clone.1 | loop fusion | flops 2353152 | bytes 1122304 | tf_op jit(solution)/shard_map/while/body/eval_jaxpr/reduce_sum | solution.py:70
  39.1 1.0 %fusion.62 = f32[4,4,128,128]{3,2,1,0:T(8,128)S(1)} fusion(f32[4,4,3,128]{3,2,1,0:T(4,128)S(1)} %copy.97, f32[4,4,3,128]{3,2,1,0:T(4,128)S(1)} %copy.98), kind=kLoop, calls=%fused_computation.4.clone.1 | loop fusion | flops 2097152 | bytes 1097728 | tf_op jit(solution)/shard_map/while/body/eval_jaxpr/reduce_sum | solution.py:63
  40.5 1.9 %fusion.63 = f32[4,4,3,128]{3,2,1,0:T(4,128)S(1)} fusion(f32[4,4,128,128]{3,2,1,0:T(8,128)S(1)} %multiply_multiply_fusion.5, f32[4,4,3,128]{3,2,1,0:T(4,128)S(1)} %copy.97, f32[4,4,3,128]{3,2,1,0:T(4,128)S(1)} %copy.98), kind=kLoop, calls=%fused_computation.5.clone.1 | loop fusion | flops 2353152 | bytes 1122304 | tf_op jit(solution)/shard_map/while/body/eval_jaxpr/reduce_sum | solution.py:70
  42.5 1.0 %fusion.62 = f32[4,4,128,128]{3,2,1,0:T(8,128)S(1)} fusion(f32[4,4,3,128]{3,2,1,0:T(4,128)S(1)} %copy.97, f32[4,4,3,128]{3,2,1,0:T(4,128)S(1)} %copy.98), kind=kLoop, calls=%fused_computation.4.clone.1 | loop fusion | flops 2097152 | bytes 1097728 | tf_op jit(solution)/shard_map/while/body/eval_jaxpr/reduce_sum | solution.py:63
  43.9 1.9 %fusion.63 = f32[4,4,3,128]{3,2,1,0:T(4,128)S(1)} fusion(f32[4,4,128,128]{3,2,1,0:T(8,128)S(1)} %multiply_multiply_fusion.5, f32[4,4,3,128]{3,2,1,0:T(4,128)S(1)} %copy.97, f32[4,4,3,128]{3,2,1,0:T(4,128)S(1)} %copy.98), kind=kLoop, calls=%fused_computation.5.clone.1 | loop fusion | flops 2353152 | bytes 1122304 | tf_op jit(solution)/shard_map/while/body/eval_jaxpr/reduce_sum | solution.py:70
  45.9 1.0 %fusion.62 = f32[4,4,128,128]{3,2,1,0:T(8,128)S(1)} fusion(f32[4,4,3,128]{3,2,1,0:T(4,128)S(1)} %copy.97, f32[4,4,3,128]{3,2,1,0:T(4,128)S(1)} %copy.98), kind=kLoop, calls=%fused_computation.4.clone.1 | loop fusion | flops 2097152 | bytes 1097728 | tf_op jit(solution)/shard_map/while/body/eval_jaxpr/reduce_sum | solution.py:63
  47.3 1.9 %fusion.63 = f32[4,4,3,128]{3,2,1,0:T(4,128)S(1)} fusion(f32[4,4,128,128]{3,2,1,0:T(8,128)S(1)} %multiply_multiply_fusion.5, f32[4,4,3,128]{3,2,1,0:T(4,128)S(1)} %copy.97, f32[4,4,3,128]{3,2,1,0:T(4,128)S(1)} %copy.98), kind=kLoop, calls=%fused_computation.5.clone.1 | loop fusion | flops 2353152 | bytes 1122304 | tf_op jit(solution)/shard_map/while/body/eval_jaxpr/reduce_sum | solution.py:70
  49.3 1.0 %fusion.62 = f32[4,4,128,128]{3,2,1,0:T(8,128)S(1)} fusion(f32[4,4,3,128]{3,2,1,0:T(4,128)S(1)} %copy.97, f32[4,4,3,128]{3,2,1,0:T(4,128)S(1)} %copy.98), kind=kLoop, calls=%fused_computation.4.clone.1 | loop fusion | flops 2097152 | bytes 1097728 | tf_op jit(solution)/shard_map/while/body/eval_jaxpr/reduce_sum | solution.py:63
  50.7 1.9 %fusion.63 = f32[4,4,3,128]{3,2,1,0:T(4,128)S(1)} fusion(f32[4,4,128,128]{3,2,1,0:T(8,128)S(1)} %multiply_multiply_fusion.5, f32[4,4,3,128]{3,2,1,0:T(4,128)S(1)} %copy.97, f32[4,4,3,128]{3,2,1,0:T(4,128)S(1)} %copy.98), kind=kLoop, calls=%fused_computation.5.clone.1 | loop fusion | flops 2353152 | bytes 1122304 | tf_op jit(solution)/shard_map/while/body/eval_jaxpr/reduce_sum | solution.py:70
  52.9 0.9 copy.76
  53.8 1.9 %reshape.243 = f32[16,1,768]{2,1,0:T(1,128)} reshape(f32[1024,3,4]{2,1,0:T(4,128)S(1)} %bitcast.87) | data formatting | bytes 98304
  55.7 7.2 %all-to-all-start.1 = ((f32[16,1,768]{2,1,0:T(1,128)}), f32[16,1,768]{2,1,0:T(1,128)S(1)}, u32[]{:S(2)}, u32[]{:S(2)}) async-start(f32[16,1,768]{2,1,0:T(1,128)} %reshape.243), calls=%async_computation.1 | async-start | bytes 98304 | tf_op jit(solution)/shard_map/all_to_all | solution.py:136
  63.4 0.8 reduce.5
  64.2 1.2 %reshape.246 = f32[1024,3,4]{2,1,0:T(4,128)S(1)} reshape(f32[16,768]{1,0:T(8,128)S(1)} %reduce.5) | data formatting | bytes 98304
  65.4 0.8 copy.68
  66.2 4.2 %all-to-all-done.1 = f32[16,1,768]{2,1,0:T(1,128)S(1)} async-done(((f32[16,1,768]{2,1,0:T(1,128)}), f32[16,1,768]{2,1,0:T(1,128)S(1)}, u32[]{:S(2)}, u32[]{:S(2)}) %all-to-all-start.1) | async-done | bytes 49184 | tf_op jit(solution)/shard_map/all_to_all | solution.py:136
  70.4 0.8 reduce.4
  71.2 1.2 %reshape.244 = f32[1024,3,4]{2,1,0:T(4,128)S(1)} reshape(f32[16,768]{1,0:T(8,128)S(1)} %reduce.4) | data formatting | bytes 98304
  72.4 0.8 copy.77
  73.7 0.5 fusion.8
  74.2 0.6 broadcast_in_dim.93
  74.8 3.6 %all-to-all-start.3 = ((f32[16,1,64]{2,1,0:T(1,128)}), f32[16,1,64]{2,1,0:T(1,128)S(1)}, u32[]{:S(2)}, u32[]{:S(2)}) async-start(f32[16,1,64]{2,1,0:T(1,128)} %broadcast_in_dim.93), calls=%async_computation.3 | async-start | bytes 16384 | tf_op jit(solution)/shard_map/all_to_all | solution.py:27
  79.1 0.8 reshape.247
  79.9 5.5 %all-to-all-done.3 = f32[16,1,64]{2,1,0:T(1,128)S(1)} async-done(((f32[16,1,64]{2,1,0:T(1,128)}), f32[16,1,64]{2,1,0:T(1,128)S(1)}, u32[]{:S(2)}, u32[]{:S(2)}) %all-to-all-start.3) | async-done | bytes 4128 | tf_op jit(solution)/shard_map/all_to_all | solution.py:27
  85.4 4.0 %all-to-all-start.2 = ((f32[16,1,1536]{2,1,0:T(1,128)}), f32[16,1,1536]{2,1,0:T(1,128)S(1)}, u32[]{:S(2)}, u32[]{:S(2)}) async-start(f32[16,1,1536]{2,1,0:T(1,128)} %reshape.247), calls=%async_computation.2 | async-start | bytes 196608 | tf_op jit(solution)/shard_map/all_to_all | solution.py:143
  89.9 0.7 reduce.3
  90.5 0.7 reshape.206
  91.2 6.7 %all-to-all-done.2 = f32[16,1,1536]{2,1,0:T(1,128)S(1)} async-done(((f32[16,1,1536]{2,1,0:T(1,128)}), f32[16,1,1536]{2,1,0:T(1,128)S(1)}, u32[]{:S(2)}, u32[]{:S(2)}) %all-to-all-start.2) | async-done | bytes 98336 | tf_op jit(solution)/shard_map/all_to_all | solution.py:143
  97.9 0.9 reduce.6
  99.1 0.6 slice_bitcast_fusion.4
  (105 shorter events, 7.5 us)
Async XLA Ops:
  2.1 18.9 %copy-start.2 = (s32[32]{0:T(128)S(1)}, s32[32]{0:T(128)}, u32[]{:S(2)}) copy-start(s32[32]{0:T(128)} %param.15) | copy-start | bytes 388
  2.1 19.9 %copy-start.3 = (s32[32]{0:T(128)S(1)}, s32[32]{0:T(128)}, u32[]{:S(2)}) copy-start(s32[32]{0:T(128)} %param.16) | copy-start | bytes 388
  2.2 20.8 %copy-start = (f32[4,3,1024]{2,0,1:T(4,128)S(1)}, f32[4,3,1024]{2,0,1:T(4,128)}, u32[]{:S(2)}) copy-start(f32[4,3,1024]{2,0,1:T(4,128)} %param.11) | copy-start | bytes 147460
  2.2 20.8 %collective-permute-start = (f32[4,4,1024]{2,0,1:T(4,128)S(1)}, f32[4,4,1024]{2,0,1:T(4,128)S(1)}, u32[]{:S(2)}, u32[]{:S(2)}) collective-permute-start(f32[4,4,1024]{2,0,1:T(4,128)S(1)} %pad_maximum_fusion.3), channel_id=1, source_target_pairs={{0,1},{1,2},{2,3},{3,4},{4,5},{5,6},{6,7},{7,8},{8,9},{9,10},{10,1... | collective-permute-start | bytes 196616 | tf_op jit(solution)/shard_map/ppermute | solution.py:17
  4.4 18.6 %collective-permute-start.1 = (f32[4,4,1024]{2,0,1:T(4,128)S(1)}, f32[4,4,1024]{2,0,1:T(4,128)S(1)}, u32[]{:S(2)}, u32[]{:S(2)}) collective-permute-start(f32[4,4,1024]{2,0,1:T(4,128)S(1)} %pad_maximum_fusion.3), channel_id=1, source_target_pairs={{1,0},{2,1},{3,2},{4,3},{5,4},{6,5},{7,6},{8,7},{9,8},{10,9},{11,1... | collective-permute-start | bytes 196616 | tf_op jit(solution)/shard_map/ppermute | solution.py:20
  11.6 44.1 %all-to-all-start = ((f32[16,1,768]{2,1,0:T(1,128)}), f32[16,1,768]{2,1,0:T(1,128)S(1)}, u32[]{:S(2)}, u32[]{:S(2)}) async-start(f32[16,1,768]{2,1,0:T(1,128)} %reshape.245), calls=%async_computation | async-start | bytes 98304 | tf_op jit(solution)/shard_map/all_to_all | solution.py:115
  25.5 27.4 %copy-start.1 = (f32[4,3,1024]{2,0,1:T(4,128)S(1)}, f32[4,3,1024]{2,0,1:T(4,128)}, u32[]{:S(2)}) copy-start(f32[4,3,1024]{2,0,1:T(4,128)} %param.12) | copy-start | bytes 147460
  55.7 14.7 %all-to-all-start.1 = ((f32[16,1,768]{2,1,0:T(1,128)}), f32[16,1,768]{2,1,0:T(1,128)S(1)}, u32[]{:S(2)}, u32[]{:S(2)}) async-start(f32[16,1,768]{2,1,0:T(1,128)} %reshape.243), calls=%async_computation.1 | async-start | bytes 98304 | tf_op jit(solution)/shard_map/all_to_all | solution.py:136
  74.8 10.6 %all-to-all-start.3 = ((f32[16,1,64]{2,1,0:T(1,128)}), f32[16,1,64]{2,1,0:T(1,128)S(1)}, u32[]{:S(2)}, u32[]{:S(2)}) async-start(f32[16,1,64]{2,1,0:T(1,128)} %broadcast_in_dim.93), calls=%async_computation.3 | async-start | bytes 16384 | tf_op jit(solution)/shard_map/all_to_all | solution.py:27
  85.4 12.5 %all-to-all-start.2 = ((f32[16,1,1536]{2,1,0:T(1,128)}), f32[16,1,1536]{2,1,0:T(1,128)S(1)}, u32[]{:S(2)}, u32[]{:S(2)}) async-start(f32[16,1,1536]{2,1,0:T(1,128)} %reshape.247), calls=%async_computation.2 | async-start | bytes 196608 | tf_op jit(solution)/shard_map/all_to_all | solution.py:143
where the time goes:
time: 100 us; the launch traced here: 99.7 us
  other arithmetic  31.7 us (32%)
  starting transfers between devices  30.2 us (30%)
  local copies, waits for them, and re-layouts  17.5 us (18%)
  waiting for transfers between devices  16.3 us (16%)
  matrix products  1.72 us (2%)
  between operations  1.68 us (2%)
    reduce_sum x8, other arithmetic, pair_force(): return jnp.sum(separation * weights[..., None, :, :], axis=-1)  14.9 us
    all_to_all x1, starting transfers between devices, on_device(): lax.all_to_all(positions, 'bead', split_axis=2, concat_axis=0, tiled=True)  9.48 us
    unnamed x15, local copies, waits for them, and re-layouts  8.81 us
    reduce_sum x8, other arithmetic, pair_force(): dist_sq = jnp.sum(separation * separation, axis=-3)  8.35 us
    all_to_all x1, starting transfers between devices, on_device(): lax.all_to_all(kicked, 'bead', split_axis=2, concat_axis=0, tiled=True)  7.23 us
    all_to_all x1, waiting for transfers between devices, on_device(): lax.all_to_all(returned_rows, 'bead', split_axis=0, concat_axis=3, tiled=...  6.67 us
    all_to_all x1, waiting for transfers between devices, sent_to_all(): lax.all_to_all(jnp.broadcast_to(x[None], (peers, *x.shape)), axis, 0, 0,...  5.48 us
    all_to_all x1, waiting for transfers between devices, on_device(): lax.all_to_all(kicked, 'bead', split_axis=2, concat_axis=0, tiled=True)  4.17 us
  transfers between devices with their start and end apart: 6, of which 3 were waited for; matrix products, arithmetic and copies ran while one was open for 43% of the time, Pallas kernels for 0%

commit v1 on v0

v1 whole, which is shorter than its diff:
```python
import functools
import math

import jax
import jax.numpy as jnp
import numpy as np
from jax import lax
from jax.experimental import pallas as pl
from jax.experimental.pallas import tpu as pltpu
from jax.sharding import PartitionSpec as P

time_step = 1.0
omega_cycle = 1.2
width_sq = 2.0

TILE = 128
BEAD_DEV = 4
TILE_DEV = 8
ATOM_DEV = TILE * TILE_DEV
ROWS = 4 * BEAD_DEV
HALF = TILE // 2
SCALE = math.log2(math.e) / (2.0 * width_sq)

VMEM = pl.BlockSpec(memory_space=pltpu.VMEM)
SMEM = pl.BlockSpec(memory_space=pltpu.SMEM)
PARAMS = pltpu.CompilerParams(vmem_limit_bytes=24 * 2**20)


def bead_tables(beads):
    j = np.arange(beads, dtype=np.float64)
    k = np.arange(beads, dtype=np.float64)
    angle = 2.0 * np.pi * j[:, None] * k[None, :] / beads
    middle = beads // 2
    table = np.where(
        k[None, :] == 0,
        np.sqrt(1.0 / beads),
        np.where(
            k[None, :] < middle,
            np.sqrt(2.0 / beads) * np.cos(angle),
            np.where(
                k[None, :] == middle,
                np.sqrt(1.0 / beads) * np.cos(np.pi * j[:, None]),
                np.sqrt(2.0 / beads) * np.sin(angle),
            ),
        ),
    )
    omega = 2.0 * omega_cycle * np.sin(np.pi * k / beads)
    sine = np.sin(omega * time_step)
    reach = np.where(omega > 0, sine / np.where(omega > 0, omega, 1.0), time_step)
    parts = (np.cos(omega * time_step), reach, -omega * sine)
    used = np.diag([1.0, 1.0, 1.0, 0.0])
    return [
        np.kron((table * part[None, :]) @ table.T, used).astype(np.float32)
        for part in parts
    ]


def component(shape):
    return lax.broadcasted_iota(jnp.int32, shape, 0) % 4


def pack_kernel(pos_ref, charge_ref, out_ref):
    for bead in range(BEAD_DEV):
        out_ref[4 * bead : 4 * bead + 3, :] = pos_ref[bead]
        out_ref[4 * bead + 3 : 4 * bead + 4, :] = charge_ref[...]


def split3(x):
    high = x.astype(jnp.bfloat16).astype(jnp.float32)
    rest = x - high
    mid = rest.astype(jnp.bfloat16).astype(jnp.float32)
    return high, mid, rest - mid


def with_norm(block):
    square = block * block
    norm = pltpu.roll(square, 1, 0) + pltpu.roll(square, 2, 0) + pltpu.roll(square, 3, 0)
    return jnp.where(component(block.shape) == 3, -SCALE * norm, block)


def prepare_right(block, first, right_ref, value_ref):
    comp = component(block.shape)
    high, mid, low = split3(with_norm(block))
    ones = jnp.ones((4, ATOM_DEV), jnp.float32)
    charge = block[3:4, :]
    values = split3(charge * jnp.where(comp == 3, 1.0, block))
    for bead in range(BEAD_DEV):
        rows = slice(4 * bead, 4 * bead + 4)
        h, m, l = high[rows], mid[rows], low[rows]
        right = jnp.concatenate([h, m, l, h, m, h, ones, 0.0 * ones], 0).astype(jnp.bfloat16)
        value = jnp.concatenate([v[rows] for v in values] + [0.0 * ones], 0).astype(jnp.bfloat16)
        for tile in range(TILE_DEV):
            lanes = slice(tile * TILE, (tile + 1) * TILE)
            right_ref[first + tile, bead] = right[:, lanes]
            value_ref[first + tile, bead] = value[:, lanes]


def prepare_left(block, left_ref):
    comp = component(block.shape)
    normed = with_norm(block)
    high, mid, low = split3(jnp.where(comp == 3, normed, 2.0 * SCALE * normed))
    for bead in range(BEAD_DEV):
        rows = slice(4 * bead, 4 * bead + 4)
        h, m, l = high[rows], mid[rows], low[rows]
        last = comp[rows] == 3
        h1 = jnp.where(last, 1.0, h)
        m0 = jnp.where(last, 0.0, m)
        l0 = jnp.where(last, 0.0, l)
        norms = jnp.concatenate([h[3:4], m[3:4], l[3:4], jnp.zeros((1, ATOM_DEV), jnp.float32)], 0)
        left = jnp.concatenate([h1, h1, h1, m0, m0, l0, norms, jnp.zeros_like(h)], 0)
        for tile in range(TILE_DEV):
            lanes = slice(tile * TILE, (tile + 1) * TILE)
            left_ref[tile, bead] = left[:, lanes].T.astype(jnp.bfloat16)


def force_kernel(
    plan_ref, own_ref, low_ref, high_ref, mom_ref, mass_ref, out_ref, left_ref, right_ref, value_ref, acc_ref
):
    slots = (plan_ref.shape[0] - 1) // 2
    own = own_ref[...]
    prepare_left(own, left_ref)
    prepare_right(low_ref[...], 0, right_ref, value_ref)
    prepare_right(own, TILE_DEV, right_ref, value_ref)
    prepare_right(high_ref[...], 2 * TILE_DEV, right_ref, value_ref)
    acc_ref[...] = jnp.zeros_like(acc_ref)

    def one_slot(slot, carry):
        tile = plan_ref[slot]
        other = plan_ref[slots + slot]
        for bead in range(BEAD_DEV):
            exponent = jnp.dot(left_ref[tile, bead], right_ref[other, bead], preferred_element_type=jnp.float32)
            weight = jnp.exp2(exponent)
            weight_high = weight.astype(jnp.bfloat16)
            weight_low = (weight - weight_high.astype(jnp.float32)).astype(jnp.bfloat16)
            value = value_ref[other, bead]
            dims = (((1,), (1,)), ((), ()))
            acc_ref[tile, bead] += lax.dot_general(
                value, weight_high, dims, preferred_element_type=jnp.float32
            ) + lax.dot_general(value, weight_low, dims, preferred_element_type=jnp.float32)
        return carry

    lax.fori_loop(0, plan_ref[2 * slots], one_slot, 0)

    mass = mass_ref[...]
    comp = component((ROWS, TILE))
    lane = lax.broadcasted_iota(jnp.int32, (ROWS, TILE), 1)
    for tile in range(TILE_DEV):
        lanes = slice(tile * TILE, (tile + 1) * TILE)
        mass_row = mass[:, lanes]
        sums, moms = [], []
        for bead in range(BEAD_DEV):
            s = acc_ref[tile, bead]
            s = s[0:4] + s[4:8] + s[8:12]
            sums.append(own[4 * bead : 4 * bead + 4, lanes] * s[3:4] - s)
            moms.append(jnp.concatenate([mom_ref[bead, :, lanes], jnp.zeros((1, TILE), jnp.float32)], 0))
        push = jnp.concatenate(sums, 0) * (0.5 * time_step / width_sq * own[3:4, lanes])
        speed = (jnp.concatenate(moms, 0) + push) / mass_row
        speed = jnp.where(comp == 3, mass_row, speed)
        place = jnp.where(comp == 3, mass_row, own[:, lanes])
        out_ref[2 * tile] = jnp.where(lane < HALF, place, pltpu.roll(speed, HALF, 1))
        out_ref[2 * tile + 1] = jnp.where(lane < HALF, pltpu.roll(place, HALF, 1), speed)


def mode_kernel(x_ref, same_ref, drift_ref, pull_ref, out_ref):
    rows = x_ref.shape[0] * x_ref.shape[1]
    beads = rows // 4
    x = x_ref[...].reshape(rows, TILE)
    swapped = pltpu.roll(x, HALF, 1)
    lane = lax.broadcasted_iota(jnp.int32, (rows, TILE), 1)
    dot = functools.partial(jnp.dot, precision=lax.Precision.HIGHEST, preferred_element_type=jnp.float32)
    moved = dot(same_ref[...], x) + jnp.where(
        lane < HALF, dot(drift_ref[...], swapped), dot(pull_ref[...], swapped)
    )
    comp = component((rows, TILE))
    mass = x[3:4, :]
    step = jnp.where(comp == 3, 0.0, moved - pltpu.roll(moved, rows - 4, 0))
    spring = jnp.sum(step * step, axis=0, keepdims=True) * mass * (0.5 * omega_cycle * omega_cycle / beads)
    moved = jnp.where(lane < HALF, moved, moved * mass)
    out_ref[...] = jnp.where(comp == 3, spring, moved).reshape(out_ref.shape)


def unpack_kernel(y_ref, pos_ref, mom_ref, spring_ref):
    lane = lax.broadcasted_iota(jnp.int32, (ROWS, TILE), 1)
    for tile in range(TILE_DEV):
        lanes = slice(tile * TILE, (tile + 1) * TILE)
        first, second = y_ref[2 * tile], y_ref[2 * tile + 1]
        place = jnp.where(lane < HALF, first, pltpu.roll(second, HALF, 1))
        push = jnp.where(lane < HALF, pltpu.roll(first, HALF, 1), second)
        for bead in range(BEAD_DEV):
            pos_ref[bead, :, lanes] = place[4 * bead : 4 * bead + 3]
            mom_ref[bead, :, lanes] = push[4 * bead : 4 * bead + 3]
        spring_ref[:, lanes] = place[3:4]


def f32(*shape):
    return jax.ShapeDtypeStruct(shape, jnp.float32)


def pack(positions, charge):
    return pl.pallas_call(
        pack_kernel, out_shape=f32(ROWS, ATOM_DEV), in_specs=[VMEM] * 2, out_specs=VMEM, compiler_params=PARAMS
    )(positions, charge[None])


def forces(plan, own, low, high, momenta, masses, peers):
    return pl.pallas_call(
        force_kernel,
        out_shape=f32(peers, ROWS, TILE),
        in_specs=[SMEM] + [VMEM] * 5,
        out_specs=VMEM,
        scratch_shapes=[
            pltpu.VMEM((TILE_DEV, BEAD_DEV, TILE, 32), jnp.bfloat16),
            pltpu.VMEM((3 * TILE_DEV, BEAD_DEV, 32, TILE), jnp.bfloat16),
            pltpu.VMEM((3 * TILE_DEV, BEAD_DEV, 16, TILE), jnp.bfloat16),
            pltpu.VMEM((TILE_DEV, BEAD_DEV, 16, TILE), jnp.float32),
        ],
        compiler_params=PARAMS,
    )(plan, own, low, high, momenta, masses[None])


def propagate(x, tables):
    return pl.pallas_call(
        mode_kernel, out_shape=f32(*x.shape), in_specs=[VMEM] * 4, out_specs=VMEM, compiler_params=PARAMS
    )(x, *tables)


def unpack(y):
    return pl.pallas_call(
        unpack_kernel,
        out_shape=(f32(BEAD_DEV, 3, ATOM_DEV), f32(BEAD_DEV, 3, ATOM_DEV), f32(1, ATOM_DEV)),
        in_specs=[VMEM],
        out_specs=(VMEM,) * 3,
        compiler_params=PARAMS,
    )(y)


def slot_plan(pair_local, pair_other, pair_count, first_tile, tiles):
    tile = pair_local - first_tile
    other = (pair_other - first_tile + TILE_DEV) % tiles
    return jnp.concatenate([tile, other, pair_count])


def on_device(positions, momenta, charge, masses, pair_local, pair_other, pair_count):
    blocks = lax.axis_size("atom")
    peers = lax.axis_size("bead")
    own = pack(positions, charge)
    up = [(i, (i + 1) % blocks) for i in range(blocks)]
    down = [(target, source) for source, target in up]
    low = lax.ppermute(own, "atom", up)
    high = lax.ppermute(own, "atom", down)
    plan = slot_plan(
        pair_local, pair_other, pair_count, lax.axis_index("atom") * TILE_DEV, TILE_DEV * blocks
    )
    sent = forces(plan, own, low, high, momenta, masses, peers)
    x = lax.all_to_all(sent, "bead", 0, 0, tiled=True)
    y = propagate(x, [jnp.asarray(t) for t in bead_tables(BEAD_DEV * peers)])
    y = lax.all_to_all(y, "bead", 0, 0, tiled=True)
    new_positions, new_momenta, spring = unpack(y)
    return new_positions, new_momenta, spring[0]


def solution(mesh):
    return jax.shard_map(
        on_device,
        mesh=mesh,
        in_specs=(
            P("bead", None, "atom"),
            P("bead", None, "atom"),
            P("atom"),
            P("atom"),
            P("atom"),
            P("atom"),
            P("atom"),
        ),
        out_specs=(P("bead", None, "atom"), P("bead", None, "atom"), P("atom")),
        check_vma=False,
    )
```

time: 100 us -> 66.7 us (0.67)
  the two profiles are of different devices: /device:TPU:1 before, /device:TPU:13 now
where the time goes in v1:
time: 66.7 us; the launch traced here: 66 us
  blocking collectives  30.8 us (46%)
  Pallas kernels  27.7 us (42%)
  local copies, waits for them, and re-layouts  2.22 us (3%)
  waiting for transfers between devices  2.19 us (3%)
  starting transfers between devices  1.54 us (2%)
  between operations  1.43 us (2%)
    pallas_call x1, Pallas kernels, forces(): pl.pallas_call(force_kernel, out_shape=f32(peers, ROWS, TILE), in_specs=[...  26.1 us
    all_to_all x1, blocking collectives, on_device(): x = lax.all_to_all(sent, 'bead', 0, 0, tiled=True)  19.2 us
    all_to_all x1, blocking collectives, on_device(): y = lax.all_to_all(y, 'bead', 0, 0, tiled=True)  11.6 us
    unnamed x20, local copies, waits for them, and re-layouts  2.22 us
    ppermute x1, waiting for transfers between devices, on_device(): low = lax.ppermute(own, 'atom', up)  1.43 us
  transfers between devices with their start and end apart: 2, of which 2 were waited for; matrix products, arithmetic and copies ran while one was open for 0% of the time, Pallas kernels for 0%

profile of v1, /device:TPU:13, one launch (start us, length us, event | category | flops | bytes accessed | tf_op | source)
XLA Modules:
  0.0 66.0 jit_solution(11184506243456194188)
XLA Ops:
  0.6 0.0 copy-start.4
  0.6 0.8 %copy.13.pos_ref = f32[4,3,1024]{2,1,0:T(4,128)S(1)} copy(f32[4,3,1024]{2,0,1:T(4,128)} %param.10) | data formatting | bytes 98304 | tf_op args[0]
  1.5 0.0 copy-done.4
  1.5 0.0 copy-start.5
  1.5 0.2 collective-permute-start.1
  1.8 1.3 %collective-permute-start = (f32[16,1024]{1,0:T(8,128)S(1)}, f32[16,1024]{1,0:T(8,128)S(1)}, u32[]{:S(2)}, u32[]{:S(2)}) collective-permute-start(f32[16,1024]{1,0:T(8,128)S(1)} %shard_map.121.own_ref), channel_id=1, source_target_pairs={{0,1},{1,2},{2,3},{3,4},{4,5},{5,6},{6,7},{7,8},{8,9},{9,10},{10,1... | collective-permute-start | bytes 196616 | tf_op jit(solution)/shard_map/ppermute | solution.py:249
  3.1 0.0 copy-start.6
  3.1 0.0 copy-start.7
  3.1 0.0 copy-start.3
  3.8 0.0 copy-done.5
  3.8 0.0 copy-start.2
  3.8 0.0 copy-done.6
  3.9 0.0 copy-done.7
  3.9 0.1 pad_add_fusion.plan_ref
  4.0 0.8 %collective-permute-done.1.high_ref = f32[16,1024]{1,0:T(8,128)S(1)} collective-permute-done((f32[16,1024]{1,0:T(8,128)S(1)}, f32[16,1024]{1,0:T(8,128)S(1)}, u32[]{:S(2)}, u32[]{:S(2)}) %collective-permute-start.1) | collective-permute-done | bytes 65568 | tf_op jit(solution)/shard_map/ppermute | solution.py:250
  4.7 1.4 %collective-permute-done.low_ref = f32[16,1024]{1,0:T(8,128)S(1)} collective-permute-done((f32[16,1024]{1,0:T(8,128)S(1)}, f32[16,1024]{1,0:T(8,128)S(1)}, u32[]{:S(2)}, u32[]{:S(2)}) %collective-permute-start) | collective-permute-done | bytes 65568 | tf_op jit(solution)/shard_map/ppermute | solution.py:249
  6.2 0.0 copy-done.3
  6.2 0.0 copy-start
  6.2 0.0 copy-start.1
  6.2 26.1 %shard_map.122 = f32[16,16,128]{2,1,0:T(8,128)S(1)} custom-call(s32[65]{0:T(128)S(1)} %pad_add_fusion.plan_ref, f32[16,1024]{1,0:T(8,128)S(1)} %shard_map.121.own_ref, f32[16,1024]{1,0:T(8,128)S(1)} %collective-permute-done.low_ref, f32[16,1024]{1,0:T(8,128)S(1)} %collective-permute-done.1.high_ref, f32[4,3,1024]{2,1,0:T(4,128)S(1)} %copy.14.mom_ref, ...), custom_call_target="tpu_custom_call" | custom-call | tf_op jit(solution)/shard_map/pallas_call | solution.py:206
  32.3 19.2 %all_to_all.10.x_ref = f32[16,16,128]{2,1,0:T(8,128)S(1)} all-to-all(f32[16,16,128]{2,1,0:T(8,128)S(1)} %shard_map.122), channel_id=1, replica_groups=mesh['bead'=16,'atom'=16] {'bead'}, dimensions={0} | all-to-all | bytes 262144 | tf_op jit(solution)/shard_map/all_to_all | solution.py:255
  51.5 0.0 copy-done.2
  51.5 0.0 copy-done
  51.5 0.0 copy-done.1
  51.5 0.9 %shard_map.123 = f32[16,16,128]{2,1,0:T(8,128)S(1)} custom-call(f32[16,16,128]{2,1,0:T(8,128)S(1)} %all_to_all.10.x_ref, f32[256,256]{1,0:T(8,128)S(1)} %copy-done.2, f32[256,256]{1,0:T(8,128)S(1)} %copy-done.1, f32[256,256]{1,0:T(8,128)S(1)} %copy-done), custom_call_target="tpu_custom_call" | custom-call | tf_op jit(solution)/shard_map/pallas_call | solution.py:222
  52.4 11.6 %all_to_all.11.y_ref = f32[16,16,128]{2,1,0:T(8,128)S(1)} all-to-all(f32[16,16,128]{2,1,0:T(8,128)S(1)} %shard_map.123), channel_id=1, replica_groups=mesh['bead'=16,'atom'=16] {'bead'}, dimensions={0} | all-to-all | bytes 262144 | tf_op jit(solution)/shard_map/all_to_all | solution.py:257
  64.0 0.7 %shard_map.124 = (f32[4,3,1024]{2,1,0:T(4,128)S(1)}, f32[4,3,1024]{2,1,0:T(4,128)S(1)}, f32[1,1024]{1,0:T(1,128)}) custom-call(f32[16,16,128]{2,1,0:T(8,128)S(1)} %all_to_all.11.y_ref), custom_call_target="tpu_custom_call" | custom-call | tf_op jit(solution)/shard_map/pallas_call | solution.py:228
  64.7 0.7 copy.15
  65.3 0.7 copy.16
  (3 shorter events, 0.1 us)
Async XLA Ops:
  0.6 0.9 %copy-start.4 = (f32[1024]{0:T(1024)S(1)}, f32[1024]{0:T(1024)}, u32[]{:S(2)}) copy-start(f32[1024]{0:T(1024)} %param.12) | copy-start | bytes 12292
  1.5 2.3 %copy-start.5 = (f32[4,3,1024]{2,0,1:T(4,128)S(1)}, f32[4,3,1024]{2,0,1:T(4,128)}, u32[]{:S(2)}) copy-start(f32[4,3,1024]{2,0,1:T(4,128)} %param.11) | copy-start | bytes 147460
  1.5 3.2 %collective-permute-start.1 = (f32[16,1024]{1,0:T(8,128)S(1)}, f32[16,1024]{1,0:T(8,128)S(1)}, u32[]{:S(2)}, u32[]{:S(2)}) collective-permute-start(f32[16,1024]{1,0:T(8,128)S(1)} %shard_map.121.own_ref), channel_id=1, source_target_pairs={{1,0},{2,1},{3,2},{4,3},{5,4},{6,5},{7,6},{8,7},{9,8},{10,9},{11,1... | collective-permute-start | bytes 196616 | tf_op jit(solution)/shard_map/ppermute | solution.py:250
  1.8 4.4 %collective-permute-start = (f32[16,1024]{1,0:T(8,128)S(1)}, f32[16,1024]{1,0:T(8,128)S(1)}, u32[]{:S(2)}, u32[]{:S(2)}) collective-permute-start(f32[16,1024]{1,0:T(8,128)S(1)} %shard_map.121.own_ref), channel_id=1, source_target_pairs={{0,1},{1,2},{2,3},{3,4},{4,5},{5,6},{6,7},{7,8},{8,9},{9,10},{10,1... | collective-permute-start | bytes 196616 | tf_op jit(solution)/shard_map/ppermute | solution.py:249
  3.1 0.8 %copy-start.6 = (s32[32]{0:T(128)S(1)}, s32[32]{0:T(128)}, u32[]{:S(2)}) copy-start(s32[32]{0:T(128)} %param.15) | copy-start | bytes 388
  3.1 0.8 %copy-start.7 = (s32[32]{0:T(128)S(1)}, s32[32]{0:T(128)}, u32[]{:S(2)}) copy-start(s32[32]{0:T(128)} %param.14) | copy-start | bytes 388
  3.1 3.1 %copy-start.3 = (f32[1024]{0:T(1024)S(1)}, f32[1024]{0:T(1024)}, u32[]{:S(2)}) copy-start(f32[1024]{0:T(1024)} %param.13) | copy-start | bytes 12292
  3.8 47.7 %copy-start.2 = (f32[256,256]{1,0:T(8,128)S(1)}, f32[256,256]{1,0:T(8,128)}, u32[]{:S(2)}) copy-start(f32[256,256]{1,0:T(8,128)} %constant.28.clone.same_ref) | copy-start | bytes 786436
  6.2 45.3 %copy-start = (f32[256,256]{1,0:T(8,128)S(1)}, f32[256,256]{1,0:T(8,128)}, u32[]{:S(2)}) copy-start(f32[256,256]{1,0:T(8,128)} %constant.30.clone.pull_ref) | copy-start | bytes 786436
  6.2 45.3 %copy-start.1 = (f32[256,256]{1,0:T(8,128)S(1)}, f32[256,256]{1,0:T(8,128)}, u32[]{:S(2)}) copy-start(f32[256,256]{1,0:T(8,128)} %constant.29.clone.drift_ref) | copy-start | bytes 786436
